TPU v7x, 32 devices: a whole 2x2x4 slice. The times are simulated.
32 devices in a mesh: groups: 2 (over y), adapter: 4 (over z), tensor: 4 (over x, core).
Axes of the slice: x: 2, y: 2, z: 4, core: 2. Of those that a mesh axis runs over, the one named last changes fastest.
Arguments:
- heads_out: bfloat16 [1024, 8192], P(('groups', 'adapter'), 'tensor'), parts along dimension 0, may hold values from -6 to 6
- out_weight: bfloat16 [8192, 8192], P('tensor', 'adapter'), may hold values from -0.0625 to 0.0625
- adapter_ids: int32 [1024], P(('groups', 'adapter')), parts along dimension 0, may hold values from 0 to 31, as said below
- shrink_weight: bfloat16 [64, 64, 8192], P(('groups', 'adapter'), None, 'tensor'), parts along dimension 0, may hold values from -0.0625 to 0.0625
- expand_weight: bfloat16 [64, 64, 8192], P(('groups', 'adapter'), None, 'tensor'), parts along dimension 0, may hold values from -0.75 to 0.75
Outputs:
- mixed: bfloat16 [1024, 8192], P(('groups', 'adapter', 'tensor')), parts along dimension 0
There are 2 independent parts, one for each index of `groups`. A program takes and returns all parts, laid end to end along the dimension named above; an argument that names none is the same for every part. Nothing has to cross between parts.
Inputs may be any that keep to these rules, and one draw needn't show every extreme that they name: `adapter_ids`: among the 128 requests on one index of the adapter axis, at most 32 use adapters held by one owner (adapters k * 8 to (k + 1) * 8 - 1 are held by index k); in every draw one owner gets exactly 32 from every index.
All inputs are finite; a program needn't handle non-finite values.
Results may differ from a plain program's by a relative error of at most 0.0053.
Values may be sent and summed in bfloat16 or wider, within the bound.
A program may use at most 128 MiB of HBM per device.

v0:
```python
import jax
import jax.numpy as jnp
from jax import lax
from jax.sharding import PartitionSpec as P


def local(heads_out, out_weight, adapter_ids, shrink_weight, expand_weight):
    owners = lax.axis_size("adapter")
    quarters = lax.axis_size("tensor")
    rows, width = heads_out.shape
    local_count = shrink_weight.shape[0]
    columns = out_weight.shape[1]
    capacity = max(2, max(rows // 8, (rows + owners - 1) // owners))
    partial_value = jnp.dot(
        lax.all_gather(heads_out, "adapter", axis=0, tiled=True),
        out_weight,
        preferred_element_type=jnp.float32,
    )
    share_rows = rows // quarters
    ordered = partial_value.reshape(owners, quarters, share_rows, columns).transpose(1, 0, 2, 3)
    ordered = ordered.reshape(quarters * owners * share_rows, columns)
    summed = lax.psum(ordered, "tensor")
    mine = lax.dynamic_slice_in_dim(
        summed, lax.axis_index("tensor") * (owners * share_rows), owners * share_rows, 0
    )
    base = lax.all_to_all(
        mine.astype(jnp.bfloat16), "adapter", split_axis=0, concat_axis=1, tiled=True
    )
    owner = adapter_ids // local_count
    owner_hits = (owner[:, None] == jnp.arange(owners)[None, :]).astype(jnp.int32)
    position = jnp.sum(jnp.cumsum(owner_hits, 0) * owner_hits, 1) - 1
    target = owner * capacity + position
    slot_hits = target[None, :] == jnp.arange(owners * capacity)[:, None]
    slot_table = slot_hits.astype(jnp.bfloat16)
    send_rows = jnp.dot(slot_table, heads_out, preferred_element_type=jnp.float32).astype(
        jnp.bfloat16
    )
    send_rows = send_rows.reshape(owners, capacity, width)
    send_ids = (jnp.sum(jnp.where(slot_hits, adapter_ids[None, :] + 1, 0), 1) - 1).reshape(
        owners, capacity
    )
    got_rows = lax.all_to_all(send_rows, "adapter", split_axis=0, concat_axis=0, tiled=True)
    got_ids = lax.all_to_all(send_ids, "adapter", split_axis=0, concat_axis=0, tiled=True)
    valid = got_ids >= 0
    which = jnp.remainder(got_ids, local_count)
    pick = (which[None] == jnp.arange(local_count)[:, None, None]) & valid[None]
    shrink_all = jnp.einsum(
        "ncd,krd->kncr", got_rows, shrink_weight, preferred_element_type=jnp.float32
    )
    part_sum = jnp.sum(jnp.where(pick[..., None], shrink_all, 0.0), 0)
    total = lax.psum(part_sum, "tensor")
    low = (0.5 * total).astype(jnp.bfloat16)
    routed = pick[..., None].astype(jnp.bfloat16) * low[None]
    delta = jnp.einsum(
        "kncr,krd->ncd", routed, expand_weight, preferred_element_type=jnp.float32
    ).astype(jnp.bfloat16)
    returned = lax.all_to_all(delta, "adapter", split_axis=0, concat_axis=0, tiled=True)
    flat_back = returned.reshape(owners * capacity, width)
    delta_local = jnp.dot(slot_table.T, flat_back, preferred_element_type=jnp.float32).astype(
        jnp.bfloat16
    )
    spread = lax.all_to_all(delta_local, "tensor", split_axis=0, concat_axis=1, tiled=True)
    return (base.astype(jnp.float32) + spread.astype(jnp.float32)).astype(jnp.bfloat16)


def solution(mesh):
    placed = (
        P(("groups", "adapter"), "tensor"),
        P("tensor", "adapter"),
        P(("groups", "adapter")),
        P(("groups", "adapter"), None, "tensor"),
        P(("groups", "adapter"), None, "tensor"),
    )
    return jax.shard_map(
        local,
        mesh=mesh,
        in_specs=placed,
        out_specs=P(("groups", "adapter", "tensor"), None),
        check_vma=False,
    )
```

profile of v0, /device:TPU:0, one launch (start us, length us, event | category | flops | bytes accessed | tf_op | source)
XLA Modules:
  0.0 215.3 jit_solution(5138305031405537828)
XLA Ops:
  6.5 0.0 copy-start
  6.5 0.0 all-gather.2.cloned.1.call-start
  6.5 0.7 all-gather.2.cloned.1.call-update
  7.3 0.7 broadcast_add_fusion.1
  7.9 0.1 fusion.18
  8.0 0.2 reduce_window_sum.11
  8.2 0.2 select_reduce_fusion.1
  8.4 0.1 select_reduce_fusion
  8.5 0.7 sub.17
  9.2 6.3 %all-to-all-start.1 = ((s32[4,1,32]{2,1,0:T(1,128)}), s32[4,1,32]{2,1,0:T(1,128)S(1)}, u32[]{:S(2)}, u32[]{:S(2)}) async-start(s32[4,1,32]{2,1,0:T(1,128)} %bitcast.4), calls=%async_computation.1 | async-start | bytes 4096 | tf_op jit(solution)/shard_map/all_to_all | solution.py:43
  15.5 2.1 convolution_convert_fusion.1
  17.6 3.3 %all-to-all-done.1 = s32[4,1,32]{2,1,0:T(1,128)S(1)} async-done(((s32[4,1,32]{2,1,0:T(1,128)}), s32[4,1,32]{2,1,0:T(1,128)S(1)}, u32[]{:S(2)}, u32[]{:S(2)}) %all-to-all-start.1) | async-done | bytes 544 | tf_op jit(solution)/shard_map/all_to_all | solution.py:43
  20.9 3.5 %all-to-all-start.2 = ((bf16[4,32,2048]{2,1,0:T(8,128)(2,1)}), bf16[4,32,2048]{2,1,0:T(8,128)(2,1)S(1)}, u32[]{:S(2)}, u32[]{:S(2)}) async-start(bf16[4,32,2048]{2,1,0:T(8,128)(2,1)} %bitcast.6), calls=%async_computation.2 | async-start | bytes 1048576 | tf_op jit(solution)/shard_map/all_to_all | solution.py:42
  24.4 29.1 %all-to-all-done.2 = bf16[4,32,2048]{2,1,0:T(8,128)(2,1)S(1)} async-done(((bf16[4,32,2048]{2,1,0:T(8,128)(2,1)}), bf16[4,32,2048]{2,1,0:T(8,128)(2,1)S(1)}, u32[]{:S(2)}, u32[]{:S(2)}) %all-to-all-start.2) | async-done | bytes 524320 | tf_op jit(solution)/shard_map/all_to_all | solution.py:42
  53.5 2.8 %fusion.10 = f32[4,32,64]{2,1,0:T(8,128)S(1)} fusion(bf16[8,64,2048]{2,1,0:T(8,128)(2,1)} %param.8, bf16[4,32,2048]{2,1,0:T(8,128)(2,1)S(1)} %all-to-all-done.2, pred[8,4,32]{2,1,0:T(4,128)(4,1)S(1)} %get-tuple-element.8), kind=kOutput, calls=%fused_computation.9 | convolution fusion | flops 268558336 | bytes 2655232 | tf_op jit(solution)/shard_map/ncd,krd->kncr/dot_general | solution.py:47
  56.3 12.4 %all-gather.2.cloned.1.call-done = bf16[512,2048]{1,0:T(8,128)(2,1)} async-done(((bf16[128,2048]{1,0:T(8,128)(2,1)}), bf16[512,2048]{1,0:T(8,128)(2,1)}) %all-gather.2.cloned.1.call-update) | async-done | bytes 2097168 | tf_op jit(solution)/shard_map/all_gather | solution.py:15
  68.7 7.6 %fusion.24 = f32[512,2048]{1,0:T(8,128)S(1)} fusion(bf16[512,2048]{1,0:T(8,128)(2,1)} %all-gather.2.cloned.1.call-done, bf16[2048,2048]{1,0:T(8,128)(2,1)} %param.6), kind=kOutput, calls=%fused_computation.40 | convolution fusion | flops 4294967296 | bytes 14680064 | tf_op jit(solution)/shard_map/dot_general | solution.py:14
  76.3 2.2 %copy.15 = f32[4,4,32,2048]{3,2,0,1:T(8,128)} copy(f32[4,4,32,2048]{3,2,1,0:T(8,128)S(1)} %bitcast.47) | data formatting | bytes 8388608 | tf_op jit(solution)/shard_map/reshape | solution.py:20
  78.5 78.7 %all-reduce.2 = (f32[4,32,64]{2,1,0:T(8,128)S(1)}, bf16[512,2048]{1,0:T(8,128)(2,1)}) all-reduce(f32[4,32,64]{2,1,0:T(8,128)S(1)} %fusion.10, f32[512,2048]{1,0:T(8,128)} %bitcast.46), channel_id=1, replica_groups=mesh['groups'=2,'adapter'=4,'tensor'=4] {'tensor'}, use_global_device_ids=true, to_apply=%region_5.6 | all-reduce | flops 1056768 | bytes 6356992 | tf_op jit(solution)/shard_map/psum | solution.py:51
  157.2 0.0 copy-done
  157.2 1.4 fusion
  158.6 3.5 %all-to-all-start.3 = ((bf16[4,32,2048]{2,1,0:T(8,128)(2,1)}), bf16[4,32,2048]{2,1,0:T(8,128)(2,1)S(1)}, u32[]{:S(2)}, u32[]{:S(2)}) async-start(bf16[4,32,2048]{2,1,0:T(8,128)(2,1)} %fusion), calls=%async_computation.3 | async-start | bytes 1048576 | tf_op jit(solution)/shard_map/all_to_all | solution.py:57
  162.1 1.9 dynamic-slice_convert_fusion
  164.0 13.3 %all-to-all-done.3 = bf16[4,32,2048]{2,1,0:T(8,128)(2,1)S(1)} async-done(((bf16[4,32,2048]{2,1,0:T(8,128)(2,1)}), bf16[4,32,2048]{2,1,0:T(8,128)(2,1)S(1)}, u32[]{:S(2)}, u32[]{:S(2)}) %all-to-all-start.3) | async-done | bytes 524320 | tf_op jit(solution)/shard_map/all_to_all | solution.py:57
  177.3 3.5 %all-to-all-start = ((bf16[4,32,2048]{2,1,0:T(8,128)(2,1)}), bf16[4,32,2048]{2,1,0:T(8,128)(2,1)S(1)}, u32[]{:S(2)}, u32[]{:S(2)}) async-start(bf16[4,32,2048]{2,1,0:T(8,128)(2,1)} %bitcast.49), calls=%async_computation | async-start | bytes 1048576 | tf_op jit(solution)/shard_map/all_to_all | solution.py:26
  180.8 1.1 convolution_convert_fusion
  181.9 13.2 %all-to-all-done = bf16[4,32,2048]{2,1,0:T(8,128)(2,1)S(1)} async-done(((bf16[4,32,2048]{2,1,0:T(8,128)(2,1)}), bf16[4,32,2048]{2,1,0:T(8,128)(2,1)S(1)}, u32[]{:S(2)}, u32[]{:S(2)}) %all-to-all-start) | async-done | bytes 524320 | tf_op jit(solution)/shard_map/all_to_all | solution.py:26
  195.2 12.3 %all_to_all.45 = bf16[4,32,2048]{2,1,0:T(8,128)(2,1)S(1)} all-to-all(bf16[4,32,2048]{2,1,0:T(8,128)(2,1)} %bitcast.50), channel_id=1, replica_groups=mesh['groups'=2,'adapter'=4,'tensor'=4] {'tensor'}, dimensions={0} | all-to-all | bytes 1048576 | tf_op jit(solution)/shard_map/all_to_all | solution.py:62
  207.4 0.1 fusion.13
  207.6 0.8 copy.21
  (7 shorter events, 0.1 us)
Async XLA Ops:
  6.5 150.6 %copy-start = (bf16[8,64,2048]{2,1,0:T(8,128)(2,1)S(1)}, bf16[8,64,2048]{2,1,0:T(8,128)(2,1)}, u32[]{:S(2)}) copy-start(bf16[8,64,2048]{2,1,0:T(8,128)(2,1)} %param.9) | copy-start | bytes 6291460
  6.5 62.2 %all-gather.2.cloned.1.call-start = ((), (), s32[]{:S(2)}) async-start(), calls=%async_computation.5 | async-start | bytes 2621440 | tf_op jit(solution)/shard_map/all_gather | solution.py:15
  9.2 11.7 %all-to-all-start.1 = ((s32[4,1,32]{2,1,0:T(1,128)}), s32[4,1,32]{2,1,0:T(1,128)S(1)}, u32[]{:S(2)}, u32[]{:S(2)}) async-start(s32[4,1,32]{2,1,0:T(1,128)} %bitcast.4), calls=%async_computation.1 | async-start | bytes 4096 | tf_op jit(solution)/shard_map/all_to_all | solution.py:43
  20.9 32.6 %all-to-all-start.2 = ((bf16[4,32,2048]{2,1,0:T(8,128)(2,1)}), bf16[4,32,2048]{2,1,0:T(8,128)(2,1)S(1)}, u32[]{:S(2)}, u32[]{:S(2)}) async-start(bf16[4,32,2048]{2,1,0:T(8,128)(2,1)} %bitcast.6), calls=%async_computation.2 | async-start | bytes 1048576 | tf_op jit(solution)/shard_map/all_to_all | solution.py:42
  158.6 18.7 %all-to-all-start.3 = ((bf16[4,32,2048]{2,1,0:T(8,128)(2,1)}), bf16[4,32,2048]{2,1,0:T(8,128)(2,1)S(1)}, u32[]{:S(2)}, u32[]{:S(2)}) async-start(bf16[4,32,2048]{2,1,0:T(8,128)(2,1)} %fusion), calls=%async_computation.3 | async-start | bytes 1048576 | tf_op jit(solution)/shard_map/all_to_all | solution.py:57
  177.3 17.9 %all-to-all-start = ((bf16[4,32,2048]{2,1,0:T(8,128)(2,1)}), bf16[4,32,2048]{2,1,0:T(8,128)(2,1)S(1)}, u32[]{:S(2)}, u32[]{:S(2)}) async-start(bf16[4,32,2048]{2,1,0:T(8,128)(2,1)} %bitcast.49), calls=%async_computation | async-start | bytes 1048576 | tf_op jit(solution)/shard_map/all_to_all | solution.py:26
Sparse Core Ops, SparseCore 0:
  8.9 59.7 all-gather.1
where the time goes:
time: 216 us; the launch traced here: 215 us
  blocking collectives  91 us (42%)
  waiting for transfers between devices  72 us (33%)
  starting transfers between devices  16.7 us (8%)
  matrix products  15 us (7%)
  between operations  13.5 us (6%)
  local copies, waits for them, and re-layouts  5.6 us (3%)
    psum x1, blocking collectives, local(): total = lax.psum(part_sum, 'tensor')  78.7 us
    all_to_all x1, waiting for transfers between devices, local(): lax.all_to_all(send_rows, 'adapter', split_axis=0, concat_axis=0, tiled=T...  29.1 us
    all_to_all x1, waiting for transfers between devices, local(): lax.all_to_all(delta, 'adapter', split_axis=0, concat_axis=0, tiled=True)  13.3 us
    all_to_all x1, waiting for transfers between devices, local(): lax.all_to_all(mine.astype(jnp.bfloat16), 'adapter', split_axis=0, concat...  13.2 us
    all_gather x1, waiting for transfers between devices, local(): lax.all_gather(heads_out, 'adapter', axis=0, tiled=True)  12.4 us
    all_to_all x1, blocking collectives, local(): lax.all_to_all(delta_local, 'tensor', split_axis=0, concat_axis=1, tiled=...  12.3 us
    dot_general x1, matrix products, local(): jnp.dot(lax.all_gather(heads_out, 'adapter', axis=0, tiled=True), out_wei...  7.56 us
    all_to_all x1, starting transfers between devices, local(): lax.all_to_all(send_ids, 'adapter', split_axis=0, concat_axis=0, tiled=True)  6.32 us
  transfers between devices with their start and end apart: 5, of which 5 were waited for; matrix products, arithmetic and copies ran while one was open for 5% of the time, Pallas kernels for 0%

commit v1 on v0

v1 whole, which is shorter than its diff:
```python
import functools

import jax
import jax.numpy as jnp
from jax import lax
from jax.experimental import pallas as pl
from jax.experimental.pallas import tpu as pltpu
from jax.sharding import PartitionSpec as P

MESH = pl.DeviceIdType.MESH
F32 = jnp.float32
BF16 = jnp.bfloat16
LANES = 128


def kernel(
    n, tn, cap, rank,
    x_ref, w_ref, s_ref, e_ref, desc_ref, u_ref,
    out_ref,
    xall, w_v, s_v, e_v, desc_v, low_v, psend, precv, dsend, drecv, bsend, brecv, esend, erecv,
    local_sem, xsend_sem, xfwd_sem, xrecv_sem, desc_send, desc_recv, low_send, low_recv,
    p_send, p_recv, d_send, d_recv, b_send, b_recv, e_send, e_recv,
):
    z = lax.axis_index("adapter")
    t = lax.axis_index("tensor")
    rows, width = x_ref.shape
    cols = w_ref.shape[1]
    share = rows // tn
    mids = s_ref.shape[0]
    groups = mids // LANES
    tile = min(512, cols)
    wtile = min(512, width)

    def remote(src, dst, ssem, rsem, **where):
        return pltpu.make_async_remote_copy(
            src_ref=src, dst_ref=dst, send_sem=ssem, recv_sem=rsem, device_id=where, device_id_type=MESH
        )

    def zpeer(j):
        return lax.rem(z + j, n)

    def tpeer(j):
        return lax.rem(t + j, tn)

    x_load = pltpu.make_async_copy(x_ref, xall.at[z], local_sem.at[0])
    s_load = pltpu.make_async_copy(s_ref, s_v, local_sem.at[1])
    w_load = pltpu.make_async_copy(w_ref, w_v, local_sem.at[2])
    e_load = pltpu.make_async_copy(e_ref, e_v, local_sem.at[3])
    x_load.start()
    s_load.start()
    w_load.start()
    e_load.start()

    barrier = pltpu.get_barrier_semaphore()
    for j in range(1, n):
        pl.semaphore_signal(barrier, inc=1, device_id={"adapter": zpeer(j)}, device_id_type=MESH)
    for j in range(1, tn):
        pl.semaphore_signal(barrier, inc=1, device_id={"tensor": tpeer(j)}, device_id_type=MESH)
    desc_v[z] = desc_ref[z]
    pl.semaphore_wait(barrier, n - 1 + tn - 1)

    def desc_copy(j):
        peer = zpeer(j)
        return remote(desc_ref.at[peer], desc_v.at[z], desc_send.at[peer], desc_recv.at[z], adapter=peer)

    for j in range(1, n):
        desc_copy(j).start()

    def own_copy(side):
        return remote(
            x_ref, xall.at[z], xsend_sem.at[side], xrecv_sem.at[z], adapter=z + 1 if side else z - 1
        )

    def fwd_copy(b, peer):
        return remote(xall.at[b], xall.at[b], xfwd_sem.at[b], xrecv_sem.at[b], adapter=peer)

    @pl.when(z + 1 < n)
    def _():
        own_copy(1).start()

    @pl.when(z > 0)
    def _():
        own_copy(0).start()

    def block_of(s):
        m = jnp.minimum(z, n - 1 - z)
        d = (s + 1) // 2
        near = jnp.where(s % 2 == 1, z - d, z + d)
        far = jnp.where(z > n - 1 - z, z - (s - m), z + (s - m))
        return jnp.where(s <= 2 * m, near, far)

    def low_copy(b, j):
        return remote(low_v.at[b, t], low_v.at[b, t], low_send.at[b, j], low_recv.at[b, t], tensor=tpeer(j))

    def part_copy(b, j):
        peer = tpeer(j)
        return remote(psend.at[b, peer], precv.at[b, t], p_send.at[b, j], p_recv.at[b, t], tensor=peer)

    def delta_copy(b):
        return remote(dsend.at[b], drecv.at[z], d_send.at[b], d_recv.at[z], adapter=b)

    def base_copy(b):
        return remote(bsend.at[b], brecv.at[z], b_send.at[b], b_recv.at[z], adapter=b)

    def landed(ref, sem):
        return remote(ref, ref, xsend_sem.at[0], sem, tensor=tpeer(1))

    def mask_of(b):
        kk = desc_v[b, :, pl.ds(rows, LANES)].astype(F32)
        half = lax.broadcasted_iota(jnp.int32, (cap, LANES), 1) // rank
        return [kk == (half + g * (LANES // rank)).astype(F32) for g in range(groups)]

    def first(s):
        b = block_of(s)

        @pl.when(s == 0)
        def _():
            x_load.wait()
            s_load.wait()

        @pl.when(s > 0)
        def _():
            landed(xall.at[b], xrecv_sem.at[b]).wait_recv()

            @pl.when((b < z) & (z + 1 < n))
            def _():
                fwd_copy(b, z + 1).start()

            @pl.when((b > z) & (z > 0))
            def _():
                fwd_copy(b, z - 1).start()

            landed(desc_v.at[b], desc_recv.at[b]).wait_recv()

        picked = jnp.dot(
            desc_v[b, :, pl.ds(0, rows)], xall[b], preferred_element_type=F32
        ).astype(BF16)
        shrunk = lax.dot_general(
            picked, s_v[...], (((1,), (1,)), ((), ())), preferred_element_type=F32
        )
        fold = jnp.zeros((cap, LANES), F32)
        for g, hit in enumerate(mask_of(b)):
            fold = fold + jnp.where(hit, shrunk[:, g * LANES:(g + 1) * LANES], 0.0)
        low_v[b, t] = fold
        for j in range(1, tn):
            low_copy(b, j).start()

        @pl.when(s == 0)
        def _():
            w_load.wait()

        def column(i, carry):
            span = pl.ds(pl.multiple_of(i * tile, tile), tile)
            part = jnp.dot(xall[b], w_v[:, span], preferred_element_type=F32)
            for q in range(tn):
                psend[b, q, :, span] = part[q * share:(q + 1) * share].astype(BF16)
            return carry

        lax.fori_loop(0, cols // tile, column, 0)
        for j in range(1, tn):
            part_copy(b, j).start()

        @pl.when(s == 0)
        def _():
            e_load.wait()

    def second(s):
        b = block_of(s)
        for j in range(1, tn):
            peer = tpeer(j)
            landed(low_v.at[b, peer], low_recv.at[b, peer]).wait_recv()
        total = low_v[b, 0]
        for q in range(1, tn):
            total = total + low_v[b, q]
        low = 0.5 * total
        routed = jnp.concatenate([jnp.where(hit, low, 0.0) for hit in mask_of(b)], axis=1).astype(BF16)
        delta = jnp.dot(routed, e_v[...], preferred_element_type=F32).astype(BF16)

        @pl.when(b == z)
        def _():
            drecv[b] = delta

        @pl.when(b != z)
        def _():
            dsend[b] = delta
            delta_copy(b).start()

        for j in range(1, tn):
            peer = tpeer(j)
            landed(precv.at[b, peer], p_recv.at[b, peer]).wait_recv()
        acc = psend[b, t].astype(F32)
        for j in range(1, tn):
            acc = acc + precv[b, tpeer(j)].astype(F32)
        base = acc.astype(BF16)

        @pl.when(b == z)
        def _():
            brecv[b] = base

        @pl.when(b != z)
        def _():
            bsend[b] = base
            base_copy(b).start()

    def step(s, carry):
        @pl.when(s < n)
        def _():
            first(s)

        @pl.when(s > 0)
        def _():
            second(s - 1)

        return carry

    lax.fori_loop(0, n + 1, step, 0)

    for j in range(1, n):
        peer = zpeer(j)
        landed(drecv.at[peer], d_recv.at[peer]).wait_recv()

    def spread(i, carry):
        span = pl.ds(pl.multiple_of(i * wtile, wtile), wtile)
        flat = drecv[:, :, span].reshape(n * cap, wtile)
        mine = jnp.dot(u_ref[...], flat, preferred_element_type=F32).astype(BF16)
        for q in range(tn):
            esend[q, :, span] = mine[q * share:(q + 1) * share]
        return carry

    lax.fori_loop(0, width // wtile, spread, 0)

    def last_copy(j):
        peer = tpeer(j)
        return remote(esend.at[peer], erecv.at[t], e_send.at[j], e_recv.at[t], tensor=peer)

    for j in range(1, tn):
        last_copy(j).start()
    erecv[t] = esend[t]
    for j in range(1, n):
        peer = zpeer(j)
        landed(brecv.at[peer], b_recv.at[peer]).wait_recv()
    for j in range(1, tn):
        peer = tpeer(j)
        landed(erecv.at[peer], e_recv.at[peer]).wait_recv()
    for o in range(n):
        q, at = (o * cols) // width, (o * cols) % width
        out_ref[:, o * cols:(o + 1) * cols] = (
            brecv[o].astype(F32) + erecv[q, :, at:at + cols].astype(F32)
        ).astype(BF16)

    @pl.when(z + 1 < n)
    def _():
        own_copy(1).wait_send()

    @pl.when(z > 0)
    def _():
        own_copy(0).wait_send()

    def drain(b, carry):
        @pl.when((b < z) & (z + 1 < n))
        def _():
            fwd_copy(b, z + 1).wait_send()

        @pl.when((b > z) & (z > 0))
        def _():
            fwd_copy(b, z - 1).wait_send()

        @pl.when(b != z)
        def _():
            remote(desc_ref.at[b], desc_v.at[z], desc_send.at[b], desc_recv.at[z], adapter=b).wait_send()
            delta_copy(b).wait_send()
            base_copy(b).wait_send()

        for j in range(1, tn):
            low_copy(b, j).wait_send()
            part_copy(b, j).wait_send()
        return carry

    lax.fori_loop(0, n, drain, 0)
    for j in range(1, tn):
        last_copy(j).wait_send()


def local(heads_out, out_weight, adapter_ids, shrink_weight, expand_weight):
    n = lax.axis_size("adapter")
    tn = lax.axis_size("tensor")
    rows, width = heads_out.shape
    local_count, rank = shrink_weight.shape[:2]
    cols = out_weight.shape[1]
    cap = max(2, max(rows // 8, (rows + n - 1) // n))
    mids = local_count * rank
    share = rows // tn

    owner = adapter_ids // local_count
    place = jnp.arange(rows)
    same = (owner[:, None] == owner[None, :]) & (place[None, :] < place[:, None])
    target = owner * cap + jnp.sum(same.astype(jnp.int32), 1)
    hits = target[None, :] == jnp.arange(n * cap)[:, None]
    which = jnp.sum(jnp.where(hits, adapter_ids[None, :] % local_count + 1, 0), 1) - 1
    desc = jnp.concatenate(
        [hits.astype(BF16), jnp.broadcast_to(which[:, None].astype(BF16), (n * cap, LANES))], axis=1
    ).reshape(n, cap, rows + LANES)
    undo = (target[:, None] == jnp.arange(n * cap)[None, :]).astype(BF16)

    any_spec = pl.BlockSpec(memory_space=pl.ANY)
    vmem_spec = pl.BlockSpec(memory_space=pltpu.VMEM)
    dma = pltpu.SemaphoreType.DMA
    return pl.pallas_call(
        functools.partial(kernel, n, tn, cap, rank),
        out_shape=jax.ShapeDtypeStruct((share, n * cols), BF16),
        in_specs=[any_spec] * 4 + [vmem_spec] * 2,
        out_specs=vmem_spec,
        scratch_shapes=[
            pltpu.VMEM((n, rows, width), BF16),
            pltpu.VMEM((width, cols), BF16),
            pltpu.VMEM((mids, width), BF16),
            pltpu.VMEM((mids, width), BF16),
            pltpu.VMEM((n, cap, rows + LANES), BF16),
            pltpu.VMEM((n, tn, cap, LANES), F32),
            pltpu.VMEM((n, tn, share, cols), BF16),
            pltpu.VMEM((n, tn, share, cols), BF16),
            pltpu.VMEM((n, cap, width), BF16),
            pltpu.VMEM((n, cap, width), BF16),
            pltpu.VMEM((n, share, cols), BF16),
            pltpu.VMEM((n, share, cols), BF16),
            pltpu.VMEM((tn, share, width), BF16),
            pltpu.VMEM((tn, share, width), BF16),
            dma((4,)),
            dma((2,)), dma((n,)), dma((n,)),
            dma((n,)), dma((n,)),
            dma((n, tn)), dma((n, tn)),
            dma((n, tn)), dma((n, tn)),
            dma((n,)), dma((n,)),
            dma((n,)), dma((n,)),
            dma((tn,)), dma((tn,)),
        ],
        compiler_params=pltpu.CompilerParams(
            collective_id=0, has_side_effects=True, vmem_limit_bytes=52 * 1024 * 1024
        ),
        cost_estimate=pl.CostEstimate(
            flops=2 * n * rows * width * cols, bytes_accessed=2 * width * (cols + 2 * mids), transcendentals=0
        ),
    )(
        heads_out,
        out_weight,
        shrink_weight.reshape(mids, width),
        expand_weight.reshape(mids, width),
        desc,
        undo,
    )


def solution(mesh):
    placed = (
        P(("groups", "adapter"), "tensor"),
        P("tensor", "adapter"),
        P(("groups", "adapter")),
        P(("groups", "adapter"), None, "tensor"),
        P(("groups", "adapter"), None, "tensor"),
    )
    return jax.shard_map(
        local,
        mesh=mesh,
        in_specs=placed,
        out_specs=P(("groups", "adapter", "tensor"), None),
        check_vma=False,
    )
```

time: 216 us -> 83.7 us (0.39)
  the two profiles are of different devices: /device:TPU:0 before, /device:TPU:25 now
where the time goes in v1:
time: 83.7 us; the launch traced here: 83.5 us
  Pallas kernels  80.3 us (96%)
  local copies, waits for them, and re-layouts  2 us (2%)
  other arithmetic  1.15 us (1%)
    pallas_call x1, Pallas kernels, local(): pl.pallas_call(functools.partial(kernel, n, tn, cap, rank), out_shape=jax...  80.3 us
    unnamed x3, local copies, waits for them, and re-layouts  1.83 us

profile of v1, /device:TPU:25, one launch (start us, length us, event | category | flops | bytes accessed | tf_op | source)
XLA Modules:
  0.0 83.5 jit_solution(14459336778953915806)
XLA Ops:
  0.0 0.7 and_select_fusion.1
  0.7 0.2 convert_reduce_fusion
  0.9 0.1 select_reduce_fusion
  1.0 0.1 convert_element_type.24
  1.1 0.1 compare_convert_fusion
  1.2 0.1 broadcast_in_dim.16
  1.3 0.1 fusion.1.u_ref
  1.4 0.0 copy-start
  1.4 1.0 %copy-done = bf16[128,2048]{1,0:T(8,128)(2,1)S(1)} copy-done((bf16[128,2048]{1,0:T(8,128)(2,1)S(1)}, bf16[128,2048]{1,0:T(8,128)(2,1)}, u32[]{:S(2)}) %copy-start) | copy-done | bytes 524312
  2.4 80.3 %shard_map.55 = bf16[32,8192]{1,0:T(8,128)(2,1)S(1)} custom-call(bf16[128,2048]{1,0:T(8,128)(2,1)S(1)} %copy-done, bf16[2048,2048]{1,0:T(8,128)(2,1)} %w_ref.1, bf16[512,2048]{1,0:T(8,128)(2,1)} %bitcast.2, bf16[512,2048]{1,0:T(8,128)(2,1)} %bitcast.3, bf16[4,32,256]{2,1,0:T(8,128)(2,1)S(1)} %pad_maximum_fusion.desc_ref, bf16[128,128]{1,0:T(8,128)(2,1)S(1)} %fusion.1.u_ref), custom_call_target="tpu_custom_call" | custom-call | flops 4294967296 | bytes 12582912 | tf_op jit(solution)/shard_map/pallas_call | solution.py:308
  82.7 0.8 copy.7
  (4 shorter events, 0.0 us)
Async XLA Ops:
  1.4 1.0 %copy-start = (bf16[128,2048]{1,0:T(8,128)(2,1)S(1)}, bf16[128,2048]{1,0:T(8,128)(2,1)}, u32[]{:S(2)}) copy-start(bf16[128,2048]{1,0:T(8,128)(2,1)} %x_ref.1) | copy-start | bytes 1572868

commit v2 on v1

--- a/solution.py
+++ b/solution.py
@@ -82,12 +82,14 @@
     def _():
         own_copy(0).start()
 
+    inner = jnp.where(z > n - 1 - z, -1, 1)
+    paired = jnp.minimum(z, n - 1 - z)
+
     def block_of(s):
-        m = jnp.minimum(z, n - 1 - z)
         d = (s + 1) // 2
-        near = jnp.where(s % 2 == 1, z - d, z + d)
-        far = jnp.where(z > n - 1 - z, z - (s - m), z + (s - m))
-        return jnp.where(s <= 2 * m, near, far)
+        near = jnp.where(s % 2 == 1, z + inner * d, z - inner * d)
+        far = z + inner * (s - paired)
+        return jnp.where(s <= 2 * paired, near, far)
 
     def low_copy(b, j):
         return remote(low_v.at[b, t], low_v.at[b, t], low_send.at[b, j], low_recv.at[b, t], tensor=tpeer(j))
@@ -110,6 +112,20 @@
         half = lax.broadcasted_iota(jnp.int32, (cap, LANES), 1) // rank
         return [kk == (half + g * (LANES // rank)).astype(F32) for g in range(groups)]
 
+    def take(b):
+        landed(xall.at[b], xrecv_sem.at[b]).wait_recv()
+
+        @pl.when((b < z) & (z + 1 < n))
+        def _():
+            fwd_copy(b, z + 1).start()
+
+        @pl.when((b > z) & (z > 0))
+        def _():
+            fwd_copy(b, z - 1).start()
+
+    def held(s):
+        return (s > 0) & (s <= 2 * paired)
+
     def first(s):
         b = block_of(s)
 
@@ -120,15 +136,13 @@
 
         @pl.when(s > 0)
         def _():
-            landed(xall.at[b], xrecv_sem.at[b]).wait_recv()
-
-            @pl.when((b < z) & (z + 1 < n))
+            @pl.when((s > 2 * paired) | (s % 2 == 1))
             def _():
-                fwd_copy(b, z + 1).start()
-
-            @pl.when((b > z) & (z > 0))
+                take(b)
+
+            @pl.when((s < 2 * paired) & (s % 2 == 1))
             def _():
-                fwd_copy(b, z - 1).start()
+                take(block_of(s + 1))
 
             landed(desc_v.at[b], desc_recv.at[b]).wait_recv()
 
@@ -154,11 +168,15 @@
             part = jnp.dot(xall[b], w_v[:, span], preferred_element_type=F32)
             for q in range(tn):
                 psend[b, q, :, span] = part[q * share:(q + 1) * share].astype(BF16)
+            for j in range(1, tn):
+                peer = tpeer(j)
+                remote(
+                    psend.at[b, peer, :, span], precv.at[b, t, :, span],
+                    p_send.at[b, j], p_recv.at[b, t], tensor=peer,
+                ).start()
             return carry
 
         lax.fori_loop(0, cols // tile, column, 0)
-        for j in range(1, tn):
-            part_copy(b, j).start()
 
         @pl.when(s == 0)
         def _():
@@ -183,6 +201,9 @@
         @pl.when(b != z)
         def _():
             dsend[b] = delta
+
+        @pl.when((b != z) & jnp.logical_not(held(s)))
+        def _():
             delta_copy(b).start()
 
         for j in range(1, tn):
@@ -200,6 +221,9 @@
         @pl.when(b != z)
         def _():
             bsend[b] = base
+
+        @pl.when((b != z) & jnp.logical_not(held(s)))
+        def _():
             base_copy(b).start()
 
     def step(s, carry):
@@ -207,13 +231,30 @@
         def _():
             first(s)
 
+        @pl.when((s == max(n - 1, 3)) & (paired > 0))
+        def _():
+            release(1)
+
         @pl.when(s > 0)
         def _():
             second(s - 1)
 
         return carry
 
+    def release(s):
+        b = block_of(s)
+        delta_copy(b).start()
+        base_copy(b).start()
+
+    def release_all(s, carry):
+        @pl.when(held(s) & (s > 1))
+        def _():
+            release(s)
+
+        return carry
+
     lax.fori_loop(0, n + 1, step, 0)
+    lax.fori_loop(2, n, release_all, 0)
 
     for j in range(1, n):
         peer = zpeer(j)

time: 83.7 us -> 74.4 us (0.89)
  the two profiles are of different devices: /device:TPU:25 before, /device:TPU:0 now
where the time goes in v2:
time: 74.4 us; the launch traced here: 73.5 us
  Pallas kernels  70.3 us (94%)
  local copies, waits for them, and re-layouts  2 us (3%)
  other arithmetic  1.15 us (2%)
    pallas_call x1, Pallas kernels, local(): pl.pallas_call(functools.partial(kernel, n, tn, cap, rank), out_shape=jax...  70.3 us
    unnamed x3, local copies, waits for them, and re-layouts  1.83 us

profile of v2, /device:TPU:0, one launch (start us, length us, event | category | flops | bytes accessed | tf_op | source)
XLA Modules:
  0.0 73.5 jit_solution(13281366474833606642)
XLA Ops:
  0.0 0.7 and_select_fusion.1
  0.7 0.2 convert_reduce_fusion
  0.9 0.1 select_reduce_fusion
  1.0 0.1 convert_element_type.24
  1.1 0.1 compare_convert_fusion
  1.2 0.1 broadcast_in_dim.16
  1.3 0.1 fusion.1.u_ref
  1.4 0.0 copy-start
  1.4 1.0 %copy-done = bf16[128,2048]{1,0:T(8,128)(2,1)S(1)} copy-done((bf16[128,2048]{1,0:T(8,128)(2,1)S(1)}, bf16[128,2048]{1,0:T(8,128)(2,1)}, u32[]{:S(2)}) %copy-start) | copy-done | bytes 524312
  2.4 70.3 %shard_map.55 = bf16[32,8192]{1,0:T(8,128)(2,1)S(1)} custom-call(bf16[128,2048]{1,0:T(8,128)(2,1)S(1)} %copy-done, bf16[2048,2048]{1,0:T(8,128)(2,1)} %w_ref.1, bf16[512,2048]{1,0:T(8,128)(2,1)} %bitcast.2, bf16[512,2048]{1,0:T(8,128)(2,1)} %bitcast.3, bf16[4,32,256]{2,1,0:T(8,128)(2,1)S(1)} %pad_maximum_fusion.desc_ref, bf16[128,128]{1,0:T(8,128)(2,1)S(1)} %fusion.1.u_ref), custom_call_target="tpu_custom_call" | custom-call | flops 4294967296 | bytes 12582912 | tf_op jit(solution)/shard_map/pallas_call | solution.py:349
  72.7 0.8 %copy.7 = bf16[32,8192]{1,0:T(8,128)(2,1)} copy(bf16[32,8192]{1,0:T(8,128)(2,1)S(1)} %shard_map.55) | data formatting | bytes 1048576
  (4 shorter events, 0.0 us)
Async XLA Ops:
  1.4 1.0 %copy-start = (bf16[128,2048]{1,0:T(8,128)(2,1)S(1)}, bf16[128,2048]{1,0:T(8,128)(2,1)}, u32[]{:S(2)}) copy-start(bf16[128,2048]{1,0:T(8,128)(2,1)} %x_ref.1) | copy-start | bytes 1572868

commit v3 on v2

--- a/solution.py
+++ b/solution.py
@@ -11,13 +11,14 @@
 F32 = jnp.float32
 BF16 = jnp.bfloat16
 LANES = 128
+PIECES = 2
 
 
 def kernel(
-    n, tn, cap, rank,
-    x_ref, w_ref, s_ref, e_ref, desc_ref, u_ref,
+    n, tn, cap, rank, count,
+    x_ref, w_ref, s_ref, e_ref, ids_ref,
     out_ref,
-    xall, w_v, s_v, e_v, desc_v, low_v, psend, precv, dsend, drecv, bsend, brecv, esend, erecv,
+    xall, w_v, s_v, e_v, desc_ref, undo, desc_v, low_v, psend, precv, dsend, drecv, bsend, brecv, esend, erecv,
     local_sem, xsend_sem, xfwd_sem, xrecv_sem, desc_send, desc_recv, low_send, low_recv,
     p_send, p_recv, d_send, d_recv, b_send, b_recv, e_send, e_recv,
 ):
@@ -56,31 +57,56 @@
         pl.semaphore_signal(barrier, inc=1, device_id={"adapter": zpeer(j)}, device_id_type=MESH)
     for j in range(1, tn):
         pl.semaphore_signal(barrier, inc=1, device_id={"tensor": tpeer(j)}, device_id_type=MESH)
-    desc_v[z] = desc_ref[z]
     pl.semaphore_wait(barrier, n - 1 + tn - 1)
 
     def desc_copy(j):
         peer = zpeer(j)
         return remote(desc_ref.at[peer], desc_v.at[z], desc_send.at[peer], desc_recv.at[z], adapter=peer)
 
+    piece = rows // PIECES
+
+    def own_copy(side, h):
+        part = pl.ds(h * piece, piece)
+        return remote(
+            x_ref.at[part], xall.at[z, part], xsend_sem.at[side, h], xrecv_sem.at[z, h],
+            adapter=z + 1 if side else z - 1,
+        )
+
+    def fwd_copy(b, h, peer):
+        part = pl.ds(h * piece, piece)
+        return remote(xall.at[b, part], xall.at[b, part], xfwd_sem.at[b, h], xrecv_sem.at[b, h], adapter=peer)
+
+    for h in range(PIECES):
+        @pl.when(z + 1 < n)
+        def _():
+            own_copy(1, h).start()
+
+        @pl.when(z > 0)
+        def _():
+            own_copy(0, h).start()
+
+    ids = jnp.broadcast_to(ids_ref[...], (rows, rows))
+    owner = jnp.zeros((rows, rows), jnp.int32)
+    for o in range(1, n):
+        owner = owner + (ids >= o * count).astype(jnp.int32)
+    at = lax.broadcasted_iota(jnp.int32, (rows, rows), 0)
+    lane = lax.broadcasted_iota(jnp.int32, (rows, rows), 1)
+    owner_of = owner.astype(F32).T.astype(jnp.int32)
+    place = jnp.sum(((owner == owner_of) & (at < lane)).astype(F32), axis=0, keepdims=True)
+    target = owner[:1] * cap + place.astype(jnp.int32)
+    slots = n * cap
+    hits = jnp.broadcast_to(target, (slots, rows)) == lax.broadcasted_iota(jnp.int32, (slots, rows), 0)
+    inside = (ids[:1] - owner[:1] * count + 1).astype(F32)
+    which = jnp.sum(jnp.where(hits, jnp.broadcast_to(inside, (slots, rows)), 0.0), axis=1, keepdims=True) - 1.0
+    table = hits.astype(F32)
+    undo[...] = table.T.astype(BF16)
+    desc_ref[:, :, pl.ds(0, rows)] = table.astype(BF16).reshape(n, cap, rows)
+    desc_ref[:, :, pl.ds(rows, LANES)] = (
+        jnp.broadcast_to(which, (slots, LANES)).astype(BF16).reshape(n, cap, LANES)
+    )
     for j in range(1, n):
         desc_copy(j).start()
-
-    def own_copy(side):
-        return remote(
-            x_ref, xall.at[z], xsend_sem.at[side], xrecv_sem.at[z], adapter=z + 1 if side else z - 1
-        )
-
-    def fwd_copy(b, peer):
-        return remote(xall.at[b], xall.at[b], xfwd_sem.at[b], xrecv_sem.at[b], adapter=peer)
-
-    @pl.when(z + 1 < n)
-    def _():
-        own_copy(1).start()
-
-    @pl.when(z > 0)
-    def _():
-        own_copy(0).start()
+    desc_v[z] = desc_ref[z]
 
     inner = jnp.where(z > n - 1 - z, -1, 1)
     paired = jnp.minimum(z, n - 1 - z)
@@ -105,23 +131,24 @@
         return remote(bsend.at[b], brecv.at[z], b_send.at[b], b_recv.at[z], adapter=b)
 
     def landed(ref, sem):
-        return remote(ref, ref, xsend_sem.at[0], sem, tensor=tpeer(1))
+        return remote(ref, ref, local_sem.at[4], sem, tensor=tpeer(1))
 
     def mask_of(b):
         kk = desc_v[b, :, pl.ds(rows, LANES)].astype(F32)
         half = lax.broadcasted_iota(jnp.int32, (cap, LANES), 1) // rank
         return [kk == (half + g * (LANES // rank)).astype(F32) for g in range(groups)]
 
-    def take(b):
-        landed(xall.at[b], xrecv_sem.at[b]).wait_recv()
+    def take(b, h):
+        part = xall.at[b, pl.ds(h * piece, piece)]
+        landed(part, xrecv_sem.at[b, h]).wait_recv()
 
         @pl.when((b < z) & (z + 1 < n))
         def _():
-            fwd_copy(b, z + 1).start()
+            fwd_copy(b, h, z + 1).start()
 
         @pl.when((b > z) & (z > 0))
         def _():
-            fwd_copy(b, z - 1).start()
+            fwd_copy(b, h, z - 1).start()
 
     def held(s):
         return (s > 0) & (s <= 2 * paired)
@@ -136,13 +163,14 @@
 
         @pl.when(s > 0)
         def _():
-            @pl.when((s > 2 * paired) | (s % 2 == 1))
-            def _():
-                take(b)
-
-            @pl.when((s < 2 * paired) & (s % 2 == 1))
-            def _():
-                take(block_of(s + 1))
+            for h in range(PIECES):
+                @pl.when((s > 2 * paired) | (s % 2 == 1))
+                def _():
+                    take(b, h)
+
+                @pl.when((s < 2 * paired) & (s % 2 == 1))
+                def _():
+                    take(block_of(s + 1), h)
 
             landed(desc_v.at[b], desc_recv.at[b]).wait_recv()
 
@@ -182,7 +210,7 @@
         def _():
             e_load.wait()
 
-    def second(s):
+    def delta_part(s):
         b = block_of(s)
         for j in range(1, tn):
             peer = tpeer(j)
@@ -206,6 +234,8 @@
         def _():
             delta_copy(b).start()
 
+    def base_part(s):
+        b = block_of(s)
         for j in range(1, tn):
             peer = tpeer(j)
             landed(precv.at[b, peer], p_recv.at[b, peer]).wait_recv()
@@ -226,30 +256,42 @@
         def _():
             base_copy(b).start()
 
+    last = max(n - 1, 3)
+
     def step(s, carry):
         @pl.when(s < n)
         def _():
             first(s)
 
-        @pl.when((s == max(n - 1, 3)) & (paired > 0))
-        def _():
-            release(1)
+        @pl.when((s == last) & (paired > 0))
+        def _():
+            delta_copy(block_of(1)).start()
+
+        @pl.when(s < n)
+        def _():
+            delta_part(s)
+
+        @pl.when((s == last) & (paired > 0))
+        def _():
+            delta_copy(block_of(2)).start()
+            base_copy(block_of(1)).start()
 
         @pl.when(s > 0)
         def _():
-            second(s - 1)
+            base_part(s - 1)
 
         return carry
 
-    def release(s):
-        b = block_of(s)
-        delta_copy(b).start()
-        base_copy(b).start()
-
     def release_all(s, carry):
-        @pl.when(held(s) & (s > 1))
-        def _():
-            release(s)
+        @pl.when(held(s))
+        def _():
+            @pl.when(s > 2)
+            def _():
+                delta_copy(block_of(s)).start()
+
+            @pl.when(s > 1)
+            def _():
+                base_copy(block_of(s)).start()
 
         return carry
 
@@ -263,7 +305,7 @@
     def spread(i, carry):
         span = pl.ds(pl.multiple_of(i * wtile, wtile), wtile)
         flat = drecv[:, :, span].reshape(n * cap, wtile)
-        mine = jnp.dot(u_ref[...], flat, preferred_element_type=F32).astype(BF16)
+        mine = jnp.dot(undo[...], flat, preferred_element_type=F32).astype(BF16)
         for q in range(tn):
             esend[q, :, span] = mine[q * share:(q + 1) * share]
         return carry
@@ -289,22 +331,24 @@
             brecv[o].astype(F32) + erecv[q, :, at:at + cols].astype(F32)
         ).astype(BF16)
 
-    @pl.when(z + 1 < n)
-    def _():
-        own_copy(1).wait_send()
-
-    @pl.when(z > 0)
-    def _():
-        own_copy(0).wait_send()
+    for h in range(PIECES):
+        @pl.when(z + 1 < n)
+        def _():
+            own_copy(1, h).wait_send()
+
+        @pl.when(z > 0)
+        def _():
+            own_copy(0, h).wait_send()
 
     def drain(b, carry):
-        @pl.when((b < z) & (z + 1 < n))
-        def _():
-            fwd_copy(b, z + 1).wait_send()
-
-        @pl.when((b > z) & (z > 0))
-        def _():
-            fwd_copy(b, z - 1).wait_send()
+        for h in range(PIECES):
+            @pl.when((b < z) & (z + 1 < n))
+            def _():
+                fwd_copy(b, h, z + 1).wait_send()
+
+            @pl.when((b > z) & (z > 0))
+            def _():
+                fwd_copy(b, h, z - 1).wait_send()
 
         @pl.when(b != z)
         def _():
@@ -332,30 +376,21 @@
     mids = local_count * rank
     share = rows // tn
 
-    owner = adapter_ids // local_count
-    place = jnp.arange(rows)
-    same = (owner[:, None] == owner[None, :]) & (place[None, :] < place[:, None])
-    target = owner * cap + jnp.sum(same.astype(jnp.int32), 1)
-    hits = target[None, :] == jnp.arange(n * cap)[:, None]
-    which = jnp.sum(jnp.where(hits, adapter_ids[None, :] % local_count + 1, 0), 1) - 1
-    desc = jnp.concatenate(
-        [hits.astype(BF16), jnp.broadcast_to(which[:, None].astype(BF16), (n * cap, LANES))], axis=1
-    ).reshape(n, cap, rows + LANES)
-    undo = (target[:, None] == jnp.arange(n * cap)[None, :]).astype(BF16)
-
-    any_spec = pl.BlockSpec(memory_space=pl.ANY)
+    any_spec = pl.BlockSpec(memory_space=pltpu.HBM)
     vmem_spec = pl.BlockSpec(memory_space=pltpu.VMEM)
     dma = pltpu.SemaphoreType.DMA
     return pl.pallas_call(
-        functools.partial(kernel, n, tn, cap, rank),
+        functools.partial(kernel, n, tn, cap, rank, local_count),
         out_shape=jax.ShapeDtypeStruct((share, n * cols), BF16),
-        in_specs=[any_spec] * 4 + [vmem_spec] * 2,
+        in_specs=[any_spec] * 4 + [vmem_spec],
         out_specs=vmem_spec,
         scratch_shapes=[
             pltpu.VMEM((n, rows, width), BF16),
             pltpu.VMEM((width, cols), BF16),
             pltpu.VMEM((mids, width), BF16),
             pltpu.VMEM((mids, width), BF16),
+            pltpu.VMEM((n, cap, rows + LANES), BF16),
+            pltpu.VMEM((rows, n * cap), BF16),
             pltpu.VMEM((n, cap, rows + LANES), BF16),
             pltpu.VMEM((n, tn, cap, LANES), F32),
             pltpu.VMEM((n, tn, share, cols), BF16),
@@ -366,8 +401,8 @@
             pltpu.VMEM((n, share, cols), BF16),
             pltpu.VMEM((tn, share, width), BF16),
             pltpu.VMEM((tn, share, width), BF16),
-            dma((4,)),
-            dma((2,)), dma((n,)), dma((n,)),
+            dma((5,)),
+            dma((2, PIECES)), dma((n, PIECES)), dma((n, PIECES)),
             dma((n,)), dma((n,)),
             dma((n, tn)), dma((n, tn)),
             dma((n, tn)), dma((n, tn)),
@@ -386,8 +421,7 @@
         out_weight,
         shrink_weight.reshape(mids, width),
         expand_weight.reshape(mids, width),
-        desc,
-        undo,
+        adapter_ids.reshape(1, rows),
     )
 
 

time: 74.4 us -> 66.7 us (0.90)
  Pallas kernels: 70.3 us -> 63.1 us
  other arithmetic: 1.15 us -> 0 us
    pallas_call x1, Pallas kernels: 70.3 us -> 63.1 us  [local(): pl.pallas_call(functools.partial(kernel, n, tn, cap, rank, local_count),...]
    unnamed x3 -> x5, local copies, waits for them, and re-layouts: 1.83 us -> 2.49 us
where the time goes in v3:
time: 66.7 us; the launch traced here: 65.6 us
  Pallas kernels  63.1 us (95%)
  local copies, waits for them, and re-layouts  2.49 us (4%)
    pallas_call x1, Pallas kernels, local(): pl.pallas_call(functools.partial(kernel, n, tn, cap, rank, local_count),...  63.1 us
    unnamed x5, local copies, waits for them, and re-layouts  2.49 us

profile of v3, /device:TPU:0, one launch (start us, length us, event | category | flops | bytes accessed | tf_op | source)
XLA Modules:
  0.0 65.6 jit_solution(15978364958399451295)
XLA Ops:
  0.0 0.0 copy-start
  0.0 1.0 %copy-done = bf16[128,2048]{1,0:T(8,128)(2,1)S(1)} copy-done((bf16[128,2048]{1,0:T(8,128)(2,1)S(1)}, bf16[128,2048]{1,0:T(8,128)(2,1)}, u32[]{:S(2)}) %copy-start) | copy-done | bytes 524312
  1.0 0.0 copy-start.1
  1.0 0.7 copy-done.1
  1.7 63.1 %shard_map.55 = bf16[32,8192]{1,0:T(8,128)(2,1)S(1)} custom-call(bf16[128,2048]{1,0:T(8,128)(2,1)S(1)} %copy-done, bf16[2048,2048]{1,0:T(8,128)(2,1)} %w_ref.1, bf16[512,2048]{1,0:T(8,128)(2,1)} %bitcast.4, bf16[512,2048]{1,0:T(8,128)(2,1)} %bitcast.5, s32[1,128]{1,0:T(1,128)S(1)} %bitcast.3), custom_call_target="tpu_custom_call" | custom-call | flops 4294967296 | bytes 12582912 | tf_op jit(solution)/shard_map/pallas_call | solution.py:382
  64.9 0.8 %copy.7 = bf16[32,8192]{1,0:T(8,128)(2,1)} copy(bf16[32,8192]{1,0:T(8,128)(2,1)S(1)} %shard_map.55) | data formatting | bytes 1048576
Async XLA Ops:
  0.0 1.0 %copy-start = (bf16[128,2048]{1,0:T(8,128)(2,1)S(1)}, bf16[128,2048]{1,0:T(8,128)(2,1)}, u32[]{:S(2)}) copy-start(bf16[128,2048]{1,0:T(8,128)(2,1)} %x_ref.1) | copy-start | bytes 1572868
  1.0 0.7 copy-start.1

commit v4 on v3

--- a/solution.py
+++ b/solution.py
@@ -266,15 +266,12 @@
         @pl.when((s == last) & (paired > 0))
         def _():
             delta_copy(block_of(1)).start()
-
-        @pl.when(s < n)
-        def _():
-            delta_part(s)
-
-        @pl.when((s == last) & (paired > 0))
-        def _():
             delta_copy(block_of(2)).start()
             base_copy(block_of(1)).start()
+
+        @pl.when(s < n)
+        def _():
+            delta_part(s)
 
         @pl.when(s > 0)
         def _():

time: 66.7 us -> 64.5 us (0.967); the launches traced: 65.6 us -> 64.4 us
  Pallas kernels: 63.1 us -> 61.9 us
    pallas_call x1, Pallas kernels: 63.1 us -> 61.9 us  [local(): pl.pallas_call(functools.partial(kernel, n, tn, cap, rank, local_count),...]
where the time goes in v4:
time: 64.5 us; the launch traced here: 64.4 us
  Pallas kernels  61.9 us (96%)
  local copies, waits for them, and re-layouts  2.49 us (4%)
    pallas_call x1, Pallas kernels, local(): pl.pallas_call(functools.partial(kernel, n, tn, cap, rank, local_count),...  61.9 us
    unnamed x5, local copies, waits for them, and re-layouts  2.49 us

profile of v4, /device:TPU:0, one launch (start us, length us, event | category | flops | bytes accessed | tf_op | source)
XLA Modules:
  0.0 64.4 jit_solution(3390383742914993891)
XLA Ops:
  0.0 0.0 copy-start
  0.0 1.0 %copy-done = bf16[128,2048]{1,0:T(8,128)(2,1)S(1)} copy-done((bf16[128,2048]{1,0:T(8,128)(2,1)S(1)}, bf16[128,2048]{1,0:T(8,128)(2,1)}, u32[]{:S(2)}) %copy-start) | copy-done | bytes 524312
  1.0 0.0 copy-start.1
  1.0 0.7 %copy-done.1 = s32[128]{0:T(128)S(1)} copy-done((s32[128]{0:T(128)S(1)}, s32[128]{0:T(128)}, u32[]{:S(2)}) %copy-start.1) | copy-done | bytes 536
  1.7 61.9 %shard_map.55 = bf16[32,8192]{1,0:T(8,128)(2,1)S(1)} custom-call(bf16[128,2048]{1,0:T(8,128)(2,1)S(1)} %copy-done, bf16[2048,2048]{1,0:T(8,128)(2,1)} %w_ref.1, bf16[512,2048]{1,0:T(8,128)(2,1)} %bitcast.4, bf16[512,2048]{1,0:T(8,128)(2,1)} %bitcast.5, s32[1,128]{1,0:T(1,128)S(1)} %bitcast.3), custom_call_target="tpu_custom_call" | custom-call | flops 4294967296 | bytes 12582912 | tf_op jit(solution)/shard_map/pallas_call | solution.py:379
  63.6 0.8 %copy.7 = bf16[32,8192]{1,0:T(8,128)(2,1)} copy(bf16[32,8192]{1,0:T(8,128)(2,1)S(1)} %shard_map.55) | data formatting | bytes 1048576
Async XLA Ops:
  0.0 1.0 %copy-start = (bf16[128,2048]{1,0:T(8,128)(2,1)S(1)}, bf16[128,2048]{1,0:T(8,128)(2,1)}, u32[]{:S(2)}) copy-start(bf16[128,2048]{1,0:T(8,128)(2,1)} %x_ref.1) | copy-start | bytes 1572868
  1.0 0.7 %copy-start.1 = (s32[128]{0:T(128)S(1)}, s32[128]{0:T(128)}, u32[]{:S(2)}) copy-start(s32[128]{0:T(128)} %param.7) | copy-start | bytes 1540

commit v5 on v4

--- a/solution.py
+++ b/solution.py
@@ -305,6 +305,11 @@
         mine = jnp.dot(undo[...], flat, preferred_element_type=F32).astype(BF16)
         for q in range(tn):
             esend[q, :, span] = mine[q * share:(q + 1) * share]
+        for j in range(1, tn):
+            peer = tpeer(j)
+            remote(
+                esend.at[peer, :, span], erecv.at[t, :, span], e_send.at[j], e_recv.at[t], tensor=peer
+            ).start()
         return carry
 
     lax.fori_loop(0, width // wtile, spread, 0)
@@ -313,8 +318,6 @@
         peer = tpeer(j)
         return remote(esend.at[peer], erecv.at[t], e_send.at[j], e_recv.at[t], tensor=peer)
 
-    for j in range(1, tn):
-        last_copy(j).start()
     erecv[t] = esend[t]
     for j in range(1, n):
         peer = zpeer(j)

time: 64.5 us -> 64.3 us (level)
  no operation moved by 1% of the time
where the time goes in v5:
time: 64.3 us; the launch traced here: 64.1 us
  Pallas kernels  61.6 us (96%)
  local copies, waits for them, and re-layouts  2.49 us (4%)
    pallas_call x1, Pallas kernels, local(): pl.pallas_call(functools.partial(kernel, n, tn, cap, rank, local_count),...  61.6 us
    unnamed x5, local copies, waits for them, and re-layouts  2.49 us

profile of v5, /device:TPU:0, one launch (start us, length us, event | category | flops | bytes accessed | tf_op | source)
XLA Modules:
  0.0 64.1 jit_solution(3373971549542553502)
XLA Ops:
  0.0 0.0 copy-start
  0.0 1.0 %copy-done = bf16[128,2048]{1,0:T(8,128)(2,1)S(1)} copy-done((bf16[128,2048]{1,0:T(8,128)(2,1)S(1)}, bf16[128,2048]{1,0:T(8,128)(2,1)}, u32[]{:S(2)}) %copy-start) | copy-done | bytes 524312
  1.0 0.0 copy-start.1
  1.0 0.7 %copy-done.1 = s32[128]{0:T(128)S(1)} copy-done((s32[128]{0:T(128)S(1)}, s32[128]{0:T(128)}, u32[]{:S(2)}) %copy-start.1) | copy-done | bytes 536
  1.7 61.6 %shard_map.55 = bf16[32,8192]{1,0:T(8,128)(2,1)S(1)} custom-call(bf16[128,2048]{1,0:T(8,128)(2,1)S(1)} %copy-done, bf16[2048,2048]{1,0:T(8,128)(2,1)} %w_ref.1, bf16[512,2048]{1,0:T(8,128)(2,1)} %bitcast.4, bf16[512,2048]{1,0:T(8,128)(2,1)} %bitcast.5, s32[1,128]{1,0:T(1,128)S(1)} %bitcast.3), custom_call_target="tpu_custom_call" | custom-call | flops 4294967296 | bytes 12582912 | tf_op jit(solution)/shard_map/pallas_call | solution.py:382
  63.3 0.8 %copy.7 = bf16[32,8192]{1,0:T(8,128)(2,1)} copy(bf16[32,8192]{1,0:T(8,128)(2,1)S(1)} %shard_map.55) | data formatting | bytes 1048576
Async XLA Ops:
  0.0 1.0 %copy-start = (bf16[128,2048]{1,0:T(8,128)(2,1)S(1)}, bf16[128,2048]{1,0:T(8,128)(2,1)}, u32[]{:S(2)}) copy-start(bf16[128,2048]{1,0:T(8,128)(2,1)} %x_ref.1) | copy-start | bytes 1572868
  1.0 0.7 %copy-start.1 = (s32[128]{0:T(128)S(1)}, s32[128]{0:T(128)}, u32[]{:S(2)}) copy-start(s32[128]{0:T(128)} %param.7) | copy-start | bytes 1540
